TPU v7x, 32 devices: a whole 2x2x4 slice. The times are simulated.
32 devices in a mesh: dp: 16 (over z, y, core), tensor: 2 (over x).
Axes of the slice: x: 2, y: 2, z: 4, core: 2. Of those that a mesh axis runs over, the one named last changes fastest.
Arguments:
- tokens: bfloat16 [65536, 768], P('dp'), may hold values from -6 to 6
- out_grad: bfloat16 [65536, 768], P('dp'), may hold values from -6 to 6
- positions: int32 [128, 76], P('dp'), may hold values from 0 to 511, as said below
- w_query: bfloat16 [768, 768], P(None, 'tensor'), may hold values from -0.21875 to 0.21875
- b_query: float32 [768], P('tensor'), may hold values from -3 to 3
- w_key: bfloat16 [768, 768], P(None, 'tensor'), may hold values from -0.21875 to 0.21875
- w_value: bfloat16 [768, 768], P(None, 'tensor'), may hold values from -0.21875 to 0.21875
- b_value: float32 [768], P('tensor'), may hold values from -3 to 3
- w_out: bfloat16 [768, 768], P('tensor'), may hold values from -0.875 to 0.875
- b_out: float32 [768], replicated, may hold values from -3 to 3
- gain_one: float32 [768], replicated, may hold values from 0.25 to 1.75
- shift_one: float32 [768], replicated, may hold values from -3 to 3
- w_up: bfloat16 [768, 3072], P(None, 'tensor'), may hold values from -0.21875 to 0.21875
- b_up: float32 [3072], P('tensor'), may hold values from -3 to 3
- w_down: bfloat16 [3072, 768], P('tensor'), may hold values from -0.109375 to 0.109375
- b_down: float32 [768], replicated, may hold values from -3 to 3
- gain_two: float32 [768], replicated, may hold values from 0.25 to 1.75
- shift_two: float32 [768], replicated, may hold values from -3 to 3
Outputs:
- layer_out: bfloat16 [65536, 768], P('dp')
- tokens_grad: float32 [65536, 768], P('dp')
- grad_w_query: float32 [768, 768], P(None, 'tensor')
- grad_b_query: float32 [768], P('tensor')
- grad_w_key: float32 [768, 768], P(None, 'tensor')
- grad_w_value: float32 [768, 768], P(None, 'tensor')
- grad_b_value: float32 [768], P('tensor')
- grad_w_out: float32 [768, 768], P('tensor')
- grad_b_out: float32 [768], replicated
- grad_gain_one: float32 [768], replicated
- grad_shift_one: float32 [768], replicated
- grad_w_up: float32 [768, 3072], P(None, 'tensor')
- grad_b_up: float32 [3072], P('tensor')
- grad_w_down: float32 [3072, 768], P('tensor')
- grad_b_down: float32 [768], replicated
- grad_gain_two: float32 [768], replicated
- grad_shift_two: float32 [768], replicated
Inputs may be any that keep to these rules, and one draw needn't show every extreme that they name: positions may repeat within a sequence, and a position counts once; a sequence has from 1 to 76 distinct positions, and some sequence has exactly 76.
All inputs are finite; a program needn't handle non-finite values.
Results may differ from a plain program's by a relative error of at most 0.024.
Values may be sent and summed in bfloat16 or wider, within the bound.
A program may use at most 256 MiB of HBM per device.

v0:
```python
import jax
import jax.numpy as jnp
from jax import lax
from jax.sharding import PartitionSpec as P

HD = 64


NORM_EPSILON = 1e-12


def product(left, right):
    return jnp.dot(left, right, preferred_element_type=jnp.float32)


def norm_parts(summed):
    average = jnp.mean(summed, axis=-1, keepdims=True)
    centred = summed - average
    inverse = lax.rsqrt(jnp.mean(centred * centred, axis=-1, keepdims=True) + NORM_EPSILON)
    return (centred * inverse, inverse)


def norm_back(upstream, normed, inverse, gain_vector):
    scaled = upstream * gain_vector
    return inverse * (
        scaled
        - jnp.mean(scaled, axis=-1, keepdims=True)
        - normed * jnp.mean(scaled * normed, axis=-1, keepdims=True)
    )


def gelu_slope(hidden):
    return (
        0.5 * (1.0 + lax.erf(hidden * 0.7071067811865476))
        + hidden * jnp.exp(-0.5 * hidden * hidden) * 0.3989422804014327
    )


def on_device(
    tokens,
    out_grad,
    positions,
    w_query,
    b_query,
    w_key,
    w_value,
    b_value,
    w_out,
    b_out,
    gain_one,
    shift_one,
    w_up,
    b_up,
    w_down,
    b_down,
    gain_two,
    shift_two,
):
    row_count = tokens.shape[0]
    sequences = positions.shape[0]
    length = row_count // sequences
    local_width = w_query.shape[1]
    local_heads = local_width // HD
    factor = HD ** (-0.5)
    queries = (product(tokens, w_query) + b_query).astype(jnp.bfloat16)
    keys_low = product(tokens, w_key).astype(jnp.bfloat16)
    values_low = (product(tokens, w_value) + b_value).astype(jnp.bfloat16)

    def by_heads(matrix):
        return matrix.reshape(sequences, length, local_heads, HD)

    def attend(triple):
        queries_seq, keys_seq, values_seq = triple
        scores = (
            jnp.einsum("qhd,khd->hqk", queries_seq, keys_seq, preferred_element_type=jnp.float32)
            * factor
        )
        highest = jnp.max(scores, axis=-1, keepdims=True)
        expanded = jnp.exp(scores - highest)
        summed = jnp.sum(expanded, axis=-1, keepdims=True)
        weights = (expanded / summed).astype(jnp.bfloat16)
        outcome = jnp.einsum(
            "hqk,khd->qhd", weights, values_seq, preferred_element_type=jnp.float32
        )
        return (
            outcome.reshape(length, local_width).astype(jnp.bfloat16),
            (highest + jnp.log(summed))[..., 0],
        )

    attended, log_totals = lax.map(
        attend, (by_heads(queries), by_heads(keys_low), by_heads(values_low))
    )
    attended = attended.reshape(row_count, local_width)
    mixed_sum = lax.psum(product(attended, w_out).astype(jnp.bfloat16), "tensor").astype(
        jnp.float32
    )
    normed_one, inverse_one = norm_parts(tokens.astype(jnp.float32) + mixed_sum + b_out)
    layer_one = normed_one * gain_one + shift_one
    layer_low = layer_one.astype(jnp.bfloat16)
    hidden = product(layer_low, w_up) + b_up
    active = jax.nn.gelu(hidden, approximate=False).astype(jnp.bfloat16)
    down_sum = lax.psum(product(active, w_down).astype(jnp.bfloat16), "tensor").astype(jnp.float32)
    normed_two, inverse_two = norm_parts(layer_one + down_sum + b_down)
    layer_out = (normed_two * gain_two + shift_two).astype(jnp.bfloat16)
    places = lax.iota(jnp.int32, length)
    marked = jnp.any(positions[:, :, None] == places[None, None, :], axis=1).astype(jnp.float32)
    upstream = out_grad.astype(jnp.float32) * marked.reshape(row_count, 1)
    grad_gain_two = jnp.sum(upstream * normed_two, axis=0)
    grad_shift_two = jnp.sum(upstream, axis=0)
    back_two = norm_back(upstream, normed_two, inverse_two, gain_two)
    grad_b_down = jnp.sum(back_two, axis=0)
    back_low = back_two.astype(jnp.bfloat16)
    grad_w_down = jnp.einsum("rf,rd->fd", active, back_low, preferred_element_type=jnp.float32)
    active_grad = jnp.einsum("rd,fd->rf", back_low, w_down, preferred_element_type=jnp.float32)
    hidden_grad = (active_grad * gelu_slope(hidden)).astype(jnp.bfloat16)
    grad_b_up = jnp.sum(hidden_grad.astype(jnp.float32), axis=0)
    grad_w_up = jnp.einsum("rd,rf->df", layer_low, hidden_grad, preferred_element_type=jnp.float32)
    layer_part = jnp.einsum("rf,df->rd", hidden_grad, w_up, preferred_element_type=jnp.float32)
    layer_grad = back_two + lax.psum(layer_part.astype(jnp.bfloat16), "tensor").astype(jnp.float32)
    grad_gain_one = jnp.sum(layer_grad * normed_one, axis=0)
    grad_shift_one = jnp.sum(layer_grad, axis=0)
    back_one = norm_back(layer_grad, normed_one, inverse_one, gain_one)
    grad_b_out = jnp.sum(back_one, axis=0)
    back_one_low = back_one.astype(jnp.bfloat16)
    grad_w_out = jnp.einsum("rc,rd->cd", attended, back_one_low, preferred_element_type=jnp.float32)
    attended_grad = jnp.einsum(
        "rd,cd->rc", back_one_low, w_out, preferred_element_type=jnp.float32
    ).astype(jnp.bfloat16)

    def attend_back(pieces):
        queries_seq, keys_seq, values_seq, outcome_grad, log_total = pieces
        scores = (
            jnp.einsum("qhd,khd->hqk", queries_seq, keys_seq, preferred_element_type=jnp.float32)
            * factor
        )
        weights = jnp.exp(scores - log_total[..., None])
        values_part = jnp.einsum(
            "hqk,qhd->khd",
            weights.astype(jnp.bfloat16),
            outcome_grad,
            preferred_element_type=jnp.float32,
        )
        weights_grad = jnp.einsum(
            "qhd,khd->hqk", outcome_grad, values_seq, preferred_element_type=jnp.float32
        )
        scores_grad = (
            weights * (weights_grad - jnp.sum(weights * weights_grad, axis=-1, keepdims=True))
        ).astype(jnp.bfloat16)
        queries_part = (
            jnp.einsum("hqk,khd->qhd", scores_grad, keys_seq, preferred_element_type=jnp.float32)
            * factor
        )
        keys_part = (
            jnp.einsum("hqk,qhd->khd", scores_grad, queries_seq, preferred_element_type=jnp.float32)
            * factor
        )
        return (
            queries_part.reshape(length, local_width).astype(jnp.bfloat16),
            keys_part.reshape(length, local_width).astype(jnp.bfloat16),
            values_part.reshape(length, local_width).astype(jnp.bfloat16),
        )

    queries_grad, keys_grad, values_grad = lax.map(
        attend_back,
        (
            by_heads(queries),
            by_heads(keys_low),
            by_heads(values_low),
            by_heads(attended_grad),
            log_totals,
        ),
    )
    queries_grad = queries_grad.reshape(row_count, local_width)
    keys_grad = keys_grad.reshape(row_count, local_width)
    values_grad = values_grad.reshape(row_count, local_width)
    grad_b_query = jnp.sum(queries_grad.astype(jnp.float32), axis=0)
    grad_b_value = jnp.sum(values_grad.astype(jnp.float32), axis=0)
    grad_w_query = jnp.einsum("rd,rc->dc", tokens, queries_grad, preferred_element_type=jnp.float32)
    grad_w_key = jnp.einsum("rd,rc->dc", tokens, keys_grad, preferred_element_type=jnp.float32)
    grad_w_value = jnp.einsum("rd,rc->dc", tokens, values_grad, preferred_element_type=jnp.float32)
    input_part = jnp.einsum("rc,dc->rd", queries_grad, w_query, preferred_element_type=jnp.float32)
    input_part = input_part + jnp.einsum(
        "rc,dc->rd", keys_grad, w_key, preferred_element_type=jnp.float32
    )
    input_part = input_part + jnp.einsum(
        "rc,dc->rd", values_grad, w_value, preferred_element_type=jnp.float32
    )
    tokens_grad = back_one + lax.psum(input_part.astype(jnp.bfloat16), "tensor").astype(jnp.float32)
    (
        grad_w_query,
        grad_b_query,
        grad_w_key,
        grad_w_value,
        grad_b_value,
        grad_w_out,
        grad_b_out,
        grad_gain_one,
        grad_shift_one,
        grad_w_up,
        grad_b_up,
        grad_w_down,
        grad_b_down,
        grad_gain_two,
        grad_shift_two,
    ) = lax.psum(
        (
            grad_w_query,
            grad_b_query,
            grad_w_key,
            grad_w_value,
            grad_b_value,
            grad_w_out,
            grad_b_out,
            grad_gain_one,
            grad_shift_one,
            grad_w_up,
            grad_b_up,
            grad_w_down,
            grad_b_down,
            grad_gain_two,
            grad_shift_two,
        ),
        "dp",
    )
    return (
        layer_out,
        tokens_grad,
        grad_w_query,
        grad_b_query,
        grad_w_key,
        grad_w_value,
        grad_b_value,
        grad_w_out,
        grad_b_out,
        grad_gain_one,
        grad_shift_one,
        grad_w_up,
        grad_b_up,
        grad_w_down,
        grad_b_down,
        grad_gain_two,
        grad_shift_two,
    )


def solution(mesh):
    in_specs = (
        P("dp", None),
        P("dp", None),
        P("dp", None),
        P(None, "tensor"),
        P("tensor"),
        P(None, "tensor"),
        P(None, "tensor"),
        P("tensor"),
        P("tensor", None),
        P(),
        P(),
        P(),
        P(None, "tensor"),
        P("tensor"),
        P("tensor", None),
        P(),
        P(),
        P(),
    )
    out_specs = (
        P("dp", None),
        P("dp", None),
        P(None, "tensor"),
        P("tensor"),
        P(None, "tensor"),
        P(None, "tensor"),
        P("tensor"),
        P("tensor", None),
        P(),
        P(),
        P(),
        P(None, "tensor"),
        P("tensor"),
        P("tensor", None),
        P(),
        P(),
        P(),
    )
    return jax.shard_map(
        on_device, mesh=mesh, in_specs=in_specs, out_specs=out_specs, check_vma=False
    )
```

profile of v0, /device:TPU:0, one launch (start us, length us, event | category | flops | bytes accessed | tf_op | source)
XLA Modules:
  0.0 1433.3 jit_solution(6629751146379080010)
XLA Ops:
  7.3 8.2 add_convert_fusion.2
  26.3 7.9 add_convert_fusion.3
  44.9 7.9 convolution_convert_fusion.4
  65.6 58.1 %while.26 = (s32[]{:T(128)}, bf16[8,512,384]{2,1,0:T(8,128)(2,1)}, f32[8,6,512]{2,1,0:T(8,128)}, bf16[8,512,6,64]{1,3,2,0:T(8,128)(2,1)}, bf16[8,512,6,64]{1,3,2...) while((s32[]{:T(128)}, bf16[8,512,384]{2,1,0:T(8,128)(2,1)}, f32[8,6,512]{2,1,0:T(8,128)}, ...), condition=%wide.region_3.4_spmd, body=%wide.region_0.3_spmd.sunk | while | flops 417002496 | bytes 22123616 | solution.py:90
  123.6 8.2 convolution_convert_fusion.2
  132.3 155.6 %all-reduce.8.cloned.1.call-done = bf16[4096,768]{1,0:T(8,128)(2,1)} async-done(((bf16[4096,768]{1,0:T(8,128)(2,1)}), bf16[4096,768]{1,0:T(8,128)(2,1)}) %all-reduce.8.cloned.1.call-update) | async-done | bytes 6291472 | tf_op jit(solution)/shard_map/psum | solution.py:94
  287.9 6.9 fusion.65
  294.8 5.6 multiply_reduce_fusion.7
  300.4 68.2 %fusion.47 = (bf16[4096,1536]{1,0:T(8,128)(2,1)}, f32[4096,1536]{1,0:T(8,128)}) fusion(f32[1536]{0:T(1024)S(1)} %copy-done.37, bf16[768,1536]{1,0:T(8,128)(2,1)S(1)} %copy-done, f32[768]{0:T(1024)S(1)} %copy-done.33, f32[768]{0:T(1024)S(1)} %copy-done.20, f32[4096]{0:T(1024)S(1)} %add_rsqrt_fusion.1, f32[4096]{0:T(1024)S(1)} %broadcast_multiply_fusion.5, ...), kind=kOutput, calls=%fused_computation.60 | convolution fusion | flops 10107224064 | bytes 52739072 | tf_op jit(solution)/shard_map/dot_general | solution.py:13
  368.7 14.6 %convolution_convert_fusion.1 = bf16[4096,768]{1,0:T(8,128)(2,1)} fusion(bf16[4096,1536]{1,0:T(8,128)(2,1)} %get-tuple-element.266, bf16[1536,768]{1,0:T(8,128)(2,1)S(1)} %copy-done.35), kind=kOutput, calls=%fused_computation.108 | convolution fusion | flops 9666822144 | bytes 21233664 | tf_op jit(solution)/shard_map/dot_general | solution.py:13
  383.9 152.8 %all-reduce.10.cloned.1.call-done = bf16[4096,768]{1,0:T(8,128)(2,1)} async-done(((bf16[4096,768]{1,0:T(8,128)(2,1)}), bf16[4096,768]{1,0:T(8,128)(2,1)}) %all-reduce.10.cloned.1.call-update) | async-done | bytes 6291472 | tf_op jit(solution)/shard_map/psum | solution.py:102
  536.7 13.1 fusion.79
  549.8 6.2 multiply_reduce_fusion.6
  556.0 11.1 multiply_reduce_fusion.2
  567.2 7.3 subtract_multiply_fusion.1
  574.6 21.8 %convert_reduce_fusion = (f32[1536]{0:T(1024)}, bf16[4096,1536]{1,0:T(8,128)(2,1)S(1)}) fusion(f32[4096,1536]{1,0:T(8,128)} %get-tuple-element.267, f32[1536]{0:T(1024)S(1)} %copy-done.37, bf16[1536,768]{1,0:T(8,128)(2,1)S(1)} %copy-done.36, f32[4096,768]{1,0:T(8,128)} %get-tuple-element.264), kind=kOutput, calls=%fused_computation.67 | convolution fusion | flops 9748609024 | bytes 52703232 | tf_op jit(solution)/shard_map/rd,fd->rf/dot_general | solution.py:114
  600.9 12.5 convolution_convert_fusion
  614.0 19.1 %fusion.69 = f32[1536,768]{1,0:T(8,128)} fusion(bf16[4096,1536]{1,0:T(8,128)(2,1)} %get-tuple-element.266, f32[4096,768]{1,0:T(8,128)} %get-tuple-element.264), kind=kOutput, calls=%fused_computation.119 | convolution fusion | flops 9666822144 | bytes 29884416 | tf_op jit(solution)/shard_map/rf,rd->fd/dot_general | solution.py:113
  633.1 133.7 %all-reduce.12.cloned.1.call-done = bf16[4096,768]{1,0:T(8,128)(2,1)} async-done(((bf16[4096,768]{1,0:T(8,128)(2,1)}), bf16[4096,768]{1,0:T(8,128)(2,1)}) %all-reduce.12.cloned.1.call-update) | async-done | bytes 6291472 | tf_op jit(solution)/shard_map/psum | solution.py:119
  766.8 14.2 multiply_reduce_fusion.3
  781.1 10.2 fusion.78
  813.8 136.6 %while.27 = (s32[]{:T(128)}, bf16[8,512,384]{1,2,0:T(8,128)(2,1)}, bf16[8,512,384]{2,1,0:T(8,128)(2,1)}, bf16[8,512,384]{1,2,0:T(8,128)(2,1)}, bf16[8,512,6,64]{...) while((s32[]{:T(128)}, bf16[8,512,384]{1,2,0:T(8,128)(2,1)}, ...), condition=%wide.region_18.19_spmd, body=%wide.region_16.18_spmd.sunk | while | flops 1026487296 | bytes 54352004 | solution.py:163
  959.8 10.1 fusion.81
  970.0 6.3 fusion.80
  976.3 12.9 add_convert_fusion
  989.8 22.8 %fusion.72 = f32[768,1536]{1,0:T(8,128)} fusion(bf16[4096,1536]{1,0:T(8,128)(2,1)} %copy-done.39, f32[768]{0:T(1024)S(1)} %copy-done.34, f32[768]{0:T(1024)S(1)} %copy-done.21, bf16[4096,768]{1,0:T(8,128)(2,1)} %all-reduce.8.cloned.1.call-done, bf16[4096,768]{1,0:T(8,128)(2,1)} %param.22, f32[4096]{0:T(1024)S(1)} %copy-done.17, ...), kind=kOutput, calls=%fused_computation.122 | convolution fusion | flops 9691987968 | bytes 29926400 | tf_op jit(solution)/shard_map/rd,rf->df/dot_general | solution.py:117
  1012.6 6.8 convolution_bitcast_fusion.2
  1019.4 6.6 convolution_bitcast_fusion
  1038.5 61.9 %all-reduce = (f32[384]{0:T(512)}, f32[384]{0:T(512)}, f32[768]{0:T(1024)}, f32[768]{0:T(1024)}, f32[768]{0:T(1024)}, /*index=5*/f32[1536]{0:T(1024)}, f32[768]{0:T(1024)}, f32[768]{0:T(1024)}, f32[768]{0:T(1024)}) all-reduce(f32[384]{0:T(512)S(1)} %convert_reduce_fusion.2, ...), channel_id=1, replica_groups=mesh['dp'=16,'tensor'=2] {'dp'}, use_global_device_ids=true, to_apply=%region_22.23 | all-reduce | flops 6912 | bytes 55296 | tf_op jit(solution)/shard_map/psum | solution.py:205
  1100.3 42.3 %all-reduce.14.cloned.1.call-done = bf16[4096,768]{1,0:T(8,128)(2,1)} async-done(((bf16[4096,768]{1,0:T(8,128)(2,1)}), bf16[4096,768]{1,0:T(8,128)(2,1)}) %all-reduce.14.cloned.1.call-update) | async-done | bytes 6291472 | tf_op jit(solution)/shard_map/psum | solution.py:188
  1142.6 12.6 convert_add_fusion
  1155.2 253.8 %all-reduce.16.cloned.1.call-done = (f32[768,384]{0,1:T(8,128)}, f32[768,384]{0,1:T(8,128)}, f32[768,384]{0,1:T(8,128)}, f32[384,768]{1,0:T(8,128)}, f32[768,1536]{1,0:T(8,128)}, /*index=5*/f32[1536,768]{1,0:T(8,128)}) async-done(((f32[768,384]{0,1:T(8,128)}, f32[768,384]{0,1:T(8,128)}, f32[768,384]{0,1:T(8,128)}, f32[384,768]{1,0:T(8,128)}, f32[768,1536]{1,0:T(8,128)}, /*index=5*/f32[1536,768]{1,0:T(8,128)}), ...) | async-done | bytes 14155792 | tf_op jit(solution)/shard_map/psum | solution.py:205
  (288 shorter events, 297.1 us)
Async XLA Ops:
  7.2 293.2 %copy-start = (bf16[768,1536]{1,0:T(8,128)(2,1)S(1)}, bf16[768,1536]{1,0:T(8,128)(2,1)}, u32[]{:S(2)}) copy-start(bf16[768,1536]{1,0:T(8,128)(2,1)} %param.34) | copy-start | bytes 7077892
  7.2 280.7 %all-reduce.8.cloned.1.call-start = ((), (), s32[]{:S(2)}) async-start(), calls=%async_computation | async-start | bytes 12582912 | tf_op jit(solution)/shard_map/psum | solution.py:94
  15.5 10.8 copy-start.14
  15.5 10.8 copy-start.38
  123.6 164.2 %copy-start.18 = (f32[768]{0:T(1024)S(1)}, f32[768]{0:T(1024)}, u32[]{:S(2)}) copy-start(f32[768]{0:T(1024)} %param.31) | copy-start | bytes 9220
  131.8 168.6 %copy-start.20 = (f32[768]{0:T(1024)S(1)}, f32[768]{0:T(1024)}, u32[]{:S(2)}) copy-start(f32[768]{0:T(1024)} %param.32) | copy-start | bytes 9220
  131.8 168.6 %copy-start.33 = (f32[768]{0:T(1024)S(1)}, f32[768]{0:T(1024)}, u32[]{:S(2)}) copy-start(f32[768]{0:T(1024)} %param.33) | copy-start | bytes 9220
  131.8 168.6 %copy-start.37 = (f32[1536]{0:T(1024)S(1)}, f32[1536]{0:T(1024)}, u32[]{:S(2)}) copy-start(f32[1536]{0:T(1024)} %param.35) | copy-start | bytes 18436
  131.8 404.9 %all-reduce.10.cloned.1.call-start = ((), (), s32[]{:S(2)}) async-start(), calls=%async_computation.1 | async-start | bytes 12582912 | tf_op jit(solution)/shard_map/psum | solution.py:102
  300.4 480.7 %copy-start.16 = (f32[4096]{0:T(1024)}, f32[4096]{0:T(1024)S(1)}, u32[]{:S(2)}) copy-start(f32[4096]{0:T(1024)S(1)} %add_rsqrt_fusion.1) | copy-start | bytes 49156
  300.4 68.2 %copy-start.35 = (bf16[1536,768]{1,0:T(8,128)(2,1)S(1)}, bf16[1536,768]{1,0:T(8,128)(2,1)}, u32[]{:S(2)}) copy-start(bf16[1536,768]{1,0:T(8,128)(2,1)} %param.36) | copy-start | bytes 7077892
  368.6 14.9 %copy-start.31 = (s32[8,76]{1,0:T(8,128)S(1)}, s32[8,76]{1,0:T(8,128)}, u32[]{:S(2)}) copy-start(s32[8,76]{1,0:T(8,128)} %param.24) | copy-start | bytes 7300
  368.6 168.1 %copy-start.32 = (f32[768]{0:T(1024)S(1)}, f32[768]{0:T(1024)}, u32[]{:S(2)}) copy-start(f32[768]{0:T(1024)} %param.37) | copy-start | bytes 9220
  383.3 383.5 %all-reduce.12.cloned.1.call-start = ((), (), s32[]{:S(2)}) async-start(), calls=%async_computation.2 | async-start | bytes 12582912 | tf_op jit(solution)/shard_map/psum | solution.py:119
  549.8 17.4 %slice-start.2 = ((s8[12582912]{0:T(1024)(128)(4,1)}), s8[4194304]{0:T(1024)(128)(4,1)S(1)}, s32[]{:S(2)}) async-start(s8[12582912]{0:T(1024)(128)(4,1)} %bitcast.155), calls=%async_computation.7 | async-start | bytes 8388608
  549.8 17.4 %slice-start.3 = ((s8[12582912]{0:T(1024)(128)(4,1)}), s8[4194304]{0:T(1024)(128)(4,1)S(1)}, s32[]{:S(2)}) async-start(s8[12582912]{0:T(1024)(128)(4,1)} %bitcast.155), calls=%async_computation.8 | async-start | bytes 8388608
  556.0 11.2 slice-start.8
  556.0 11.2 copy-start.30
  556.0 11.2 slice-start.4
  556.0 11.2 slice-start.9
  613.5 529.1 %all-reduce.14.cloned.1.call-start = ((), (), s32[]{:S(2)}) async-start(), calls=%async_computation.3 | async-start | bytes 12582912 | tf_op jit(solution)/shard_map/psum | solution.py:188
  766.8 14.3 copy-start.8
  781.1 15.0 %copy-start.10 = (bf16[384,768]{1,0:T(8,128)(2,1)S(1)}, bf16[384,768]{1,0:T(8,128)(2,1)}, u32[]{:S(2)}) copy-start(bf16[384,768]{1,0:T(8,128)(2,1)} %param.30) | copy-start | bytes 1769476
  955.1 14.8 %copy-start.13 = (bf16[768,384]{1,0:T(8,128)(2,1)S(1)}, bf16[768,384]{1,0:T(8,128)(2,1)}, u32[]{:S(2)}) copy-start(bf16[768,384]{1,0:T(8,128)(2,1)} %param.25) | copy-start | bytes 1769476
  976.3 13.4 copy-start.17
  976.3 13.5 copy-start.19
  976.3 13.5 copy-start.21
  976.3 13.5 copy-start.34
  989.3 419.8 %all-reduce.16.cloned.1.call-start = ((), (), s32[]{:S(2)}) async-start(), calls=%async_computation.4 | async-start | bytes 28311552 | tf_op jit(solution)/shard_map/psum | solution.py:205
  989.8 22.8 %copy-start.4 = (bf16[8,512,384]{2,1,0:T(8,128)(2,1)S(1)}, bf16[8,512,384]{2,1,0:T(8,128)(2,1)}, u32[]{:S(2)}) copy-start(bf16[8,512,384]{2,1,0:T(8,128)(2,1)} %copy.88) | copy-start | bytes 9437188
  1012.6 13.5 slice-start
  1409.0 15.4 %slice-start.10 = ((s8[4718592]{0:T(1024)(128)(4,1)}), s8[524288]{0:T(1024)(128)(4,1)S(1)}, s32[]{:S(2)}) async-start(s8[4718592]{0:T(1024)(128)(4,1)} %bitcast.179), calls=%async_computation.15 | async-start | bytes 1048576
  (25 other events, 162.7 us)
Sparse Core Ops, SparseCore 0:
  131.9 155.8 all-reduce.7
  383.4 153.2 all-reduce.9
  613.6 153.1 all-reduce.11
  989.4 153.1 all-reduce.13
  1148.8 260.2 all-reduce.15
where the time goes:
time: 1440 us; the launch traced here: 1430 us
  waiting for transfers between devices  738 us (51%)
  matrix products  369 us (26%)
  local copies, waits for them, and re-layouts  127 us (9%)
  other arithmetic  121 us (8%)
  blocking collectives  61.9 us (4%)
  between operations  14.6 us (1%)
    psum x1, waiting for transfers between devices, on_device(): lax.psum((grad_w_query, grad_b_query, grad_w_key, grad_w_value, grad_b_va...  254 us
    psum x1, waiting for transfers between devices, on_device(): lax.psum(product(attended, w_out).astype(jnp.bfloat16), 'tensor')  156 us
    psum x1, waiting for transfers between devices, on_device(): lax.psum(product(active, w_down).astype(jnp.bfloat16), 'tensor')  153 us
    psum x1, waiting for transfers between devices, on_device(): lax.psum(layer_part.astype(jnp.bfloat16), 'tensor').astype(jnp.float32)  134 us
    dot_general x6, matrix products, product(): return jnp.dot(left, right, preferred_element_type=jnp.float32)  115 us
    psum x1, blocking collectives, on_device(): lax.psum((grad_w_query, grad_b_query, grad_w_key, grad_w_value, grad_b_va...  61.9 us
    psum x1, waiting for transfers between devices, on_device(): lax.psum(input_part.astype(jnp.bfloat16), 'tensor').astype(jnp.float32)  42.3 us
    unnamed x116, local copies, waits for them, and re-layouts  40.4 us
  transfers between devices with their start and end apart: 5, of which 5 were waited for; matrix products, arithmetic and copies ran while one was open for 6% of the time, Pallas kernels for 0%

commit v1 on v0

v1 whole, which is shorter than its diff:
```python
import functools
import math

import jax
import jax.numpy as jnp
from jax import lax
from jax.experimental import pallas as pl
from jax.experimental.pallas import tpu as pltpu
from jax.sharding import PartitionSpec as P

HD = 64
NORM_EPSILON = 1e-12
BF16 = jnp.bfloat16
F32 = jnp.float32
EXPONENT = HD**-0.5 * math.log2(math.e)
ROOT_HALF = 0.7071067811865476
DENSITY = 0.3989422804014327
VMEM_BYTES = 58 * 2**20


def dot(left, right):
    return jnp.dot(left, right, preferred_element_type=F32)


def dot_nt(left, right):
    return lax.dot_general(left, right, (((1,), (1,)), ((), ())), preferred_element_type=F32)


def dot_tn(left, right):
    return lax.dot_general(left, right, (((0,), (0,)), ((), ())), preferred_element_type=F32)


def norm_parts(summed):
    centred = summed - jnp.mean(summed, axis=-1, keepdims=True)
    inverse = lax.rsqrt(jnp.mean(centred * centred, axis=-1, keepdims=True) + NORM_EPSILON)
    return centred * inverse, inverse


def norm_back(upstream, normed, inverse, gain):
    scaled = upstream * gain
    return inverse * (
        scaled
        - jnp.mean(scaled, axis=-1, keepdims=True)
        - normed * jnp.mean(scaled * normed, axis=-1, keepdims=True)
    )


def row_sum(values):
    return jnp.sum(values, axis=0, keepdims=True)


def picker(slots, length):
    return jnp.where(
        slots == lax.broadcasted_iota(jnp.int32, (slots.shape[0], length), 1), 1.0, 0.0
    ).astype(BF16)


def rows_spec(rows, width):
    return pl.BlockSpec((rows, width), lambda i: (i, 0))


def whole_spec(array):
    return pl.BlockSpec(array.shape, lambda i: (0, 0), pipeline_mode=pl.Buffered(1))


def params():
    return pltpu.CompilerParams(vmem_limit_bytes=VMEM_BYTES)


def attention_body(
    tokens, w_qkv, b_query, b_value, slots, attended, keys, values, picked_q, picked_att
):
    length = tokens.shape[0]
    width = keys.shape[1]
    qkv = dot(tokens[...], w_qkv[...])
    query = (qkv[:, :width] + b_query[...]).astype(BF16)
    key = qkv[:, width : 2 * width].astype(BF16)
    value = (qkv[:, 2 * width :] + b_value[...]).astype(BF16)
    keys[...] = key
    values[...] = value
    pair = 2 * HD
    first = lax.broadcasted_iota(jnp.int32, (length, pair), 1) < HD
    zero = jnp.zeros((length, pair), BF16)
    one = jnp.ones((length, pair), BF16)
    for p in range(width // pair):
        here = slice(p * pair, (p + 1) * pair)
        k, v = key[:, here], value[:, here]
        k_two = jnp.concatenate([jnp.where(first, k, zero), jnp.where(first, zero, k)], axis=0)
        v_two = jnp.concatenate(
            [
                jnp.concatenate([jnp.where(first, v, zero), jnp.where(first, one, zero)], axis=1),
                jnp.concatenate([jnp.where(first, zero, v), jnp.where(first, zero, one)], axis=1),
            ],
            axis=0,
        )
        scores = dot_nt(query[:, here], k_two)
        left, right = scores[:, :length], scores[:, length:]
        left = jnp.exp2((left - jnp.max(left, axis=1, keepdims=True)) * EXPONENT).astype(BF16)
        right = jnp.exp2((right - jnp.max(right, axis=1, keepdims=True)) * EXPONENT).astype(BF16)
        both = dot(jnp.concatenate([left, right], axis=1), v_two)
        attended[:, here] = (both[:, :pair] / both[:, pair:]).astype(BF16)
    pick = picker(slots[...], length)
    picked_q[...] = dot(pick, query).astype(BF16)
    picked_att[...] = dot(pick, attended[...]).astype(BF16)


def attention(tokens, w_qkv, b_query, b_value, slots, sequences):
    rows, model = tokens.shape
    length = rows // sequences
    width = w_qkv.shape[1] // 3
    taken = slots.shape[0] // sequences
    shape = jax.ShapeDtypeStruct
    return pl.pallas_call(
        attention_body,
        grid=(sequences,),
        in_specs=[
            rows_spec(length, model),
            whole_spec(w_qkv),
            whole_spec(b_query),
            whole_spec(b_value),
            rows_spec(taken, 1),
        ],
        out_specs=[rows_spec(length, width)] * 3 + [rows_spec(taken, width)] * 2,
        out_shape=[shape((rows, width), BF16)] * 3 + [shape((slots.shape[0], width), BF16)] * 2,
        compiler_params=params(),
        cost_estimate=pl.CostEstimate(
            flops=int(rows * width * (6 * model + 16 * length)),
            bytes_accessed=rows * (model + 3 * width) * 2,
            transcendentals=rows * length * width // HD,
        ),
        name="attention",
    )(tokens, w_qkv, b_query, b_value, slots)


def pick_body(tokens, out_grad, slots, picked_tokens, picked_grad):
    pick = picker(slots[...], tokens.shape[0])
    picked_tokens[...] = dot(pick, tokens[...]).astype(BF16)
    picked_grad[...] = dot(pick, out_grad[...]).astype(BF16)


def pick_rows(tokens, out_grad, slots, sequences):
    rows, model = tokens.shape
    length = rows // sequences
    taken = slots.shape[0] // sequences
    return pl.pallas_call(
        pick_body,
        grid=(sequences,),
        in_specs=[rows_spec(length, model)] * 2 + [rows_spec(taken, 1)],
        out_specs=[rows_spec(taken, model)] * 2,
        out_shape=[jax.ShapeDtypeStruct((slots.shape[0], model), BF16)] * 2,
        compiler_params=params(),
        name="pick",
    )(tokens, out_grad, slots)


def gelu_share(hidden):
    return 0.5 * (1.0 + lax.erf(hidden * ROOT_HALF))


def marked_body(
    tokens,
    attended_own,
    attended_peer,
    upstream,
    w_out,
    w_up_own,
    w_up_peer,
    w_down_own,
    w_down_peer,
    b_out,
    gain_one,
    shift_one,
    b_up_own,
    b_up_peer,
    b_down,
    gain_two,
    back_one_out,
    attended_grad_own,
    attended_grad_peer,
    grad_w_up,
    grad_w_down,
    grad_w_out,
    grad_b_up,
    vectors,
    slope,
    active,
):
    width = attended_own.shape[1]
    half = w_up_own.shape[1]
    chunk = half
    attended = jnp.concatenate([attended_own[...], attended_peer[...]], axis=1)
    normed_one, inverse_one = norm_parts(
        tokens[...].astype(F32) + dot(attended, w_out[...]) + b_out[...]
    )
    layer_one = normed_one * gain_one[...] + shift_one[...]
    layer_low = layer_one.astype(BF16)
    summed = layer_one + b_down[...]
    parts = (
        (0, w_up_own, w_down_own, b_up_own),
        (half, w_up_peer, w_down_peer, b_up_peer),
    )
    for start, w_up, w_down, b_up in parts:
        for c in range(0, half, chunk):
            here = slice(c, c + chunk)
            hidden = dot(layer_low, w_up[:, here]) + b_up[:, here]
            share = gelu_share(hidden)
            act = (hidden * share).astype(BF16)
            slope[:, start + c : start + c + chunk] = (
                share + hidden * jnp.exp(-0.5 * hidden * hidden) * DENSITY
            )
            if start == 0:
                active[:, here] = act
            summed = summed + dot(act, w_down[here, :])
    normed_two, inverse_two = norm_parts(summed)
    up = upstream[...].astype(F32)
    back_two = norm_back(up, normed_two, inverse_two, gain_two[...])
    back_low = back_two.astype(BF16)
    layer_grad = back_two
    for start, w_up, w_down, b_up in parts:
        for c in range(0, half, chunk):
            here = slice(c, c + chunk)
            hidden_grad = (
                dot_nt(back_low, w_down[here, :]) * slope[:, start + c : start + c + chunk]
            ).astype(BF16)
            layer_grad = layer_grad + dot_nt(hidden_grad, w_up[:, here])
            if start == 0:
                grad_b_up[:, here] = row_sum(hidden_grad.astype(F32))
                grad_w_up[:, here] = dot_tn(layer_low, hidden_grad).astype(BF16)
                grad_w_down[here, :] = dot_tn(active[:, here], back_low).astype(BF16)
    back_one = norm_back(layer_grad, normed_one, inverse_one, gain_one[...])
    back_one_low = back_one.astype(BF16)
    back_one_out[...] = back_one
    grad_w_out[...] = dot_tn(attended_own[...], back_one_low).astype(BF16)
    attended_grad = dot_nt(back_one_low, w_out[...]).astype(BF16)
    attended_grad_own[...] = attended_grad[:, :width]
    attended_grad_peer[...] = attended_grad[:, width:]
    vectors[...] = jnp.concatenate(
        [
            row_sum(back_one),
            row_sum(layer_grad * normed_one),
            row_sum(layer_grad),
            row_sum(back_two),
            row_sum(up * normed_two),
            row_sum(up),
            jnp.zeros((2, up.shape[1]), F32),
        ],
        axis=0,
    )


def marked_rows(*args):
    tokens, attended_own = args[0], args[1]
    rows, model = tokens.shape
    width = attended_own.shape[1]
    half = args[5].shape[1]
    shape = jax.ShapeDtypeStruct
    return pl.pallas_call(
        marked_body,
        out_shape=[
            shape((rows, model), F32),
            shape((rows, width), BF16),
            shape((rows, width), BF16),
            shape((model, half), BF16),
            shape((half, model), BF16),
            shape((width, model), BF16),
            shape((1, half), F32),
            shape((8, model), F32),
        ],
        scratch_shapes=[pltpu.VMEM((rows, 2 * half), F32), pltpu.VMEM((rows, half), BF16)],
        compiler_params=params(),
        cost_estimate=pl.CostEstimate(
            flops=int(rows * model * (2 * half * 10 + 2 * width * 5)),
            bytes_accessed=6 * model * half * 2,
            transcendentals=rows * half * 4,
        ),
        name="marked",
    )(*args)


def backward_body(
    tokens,
    keys_own,
    keys_peer,
    values_own,
    values_peer,
    query_own,
    query_peer,
    grad_own,
    grad_peer,
    back_one,
    slots,
    picked_tokens,
    w_query,
    w_key_value,
    tokens_grad,
    grad_w_query,
    grad_w_key_value,
    grad_b_query,
    grad_b_value,
    query_grads,
    sums,
):
    step = pl.program_id(0)
    last = pl.num_programs(0) - 1
    length = tokens.shape[0]
    width = keys_own.shape[1]
    taken = slots.shape[0]
    factor = HD**-0.5
    pair = 2 * HD
    first = lax.broadcasted_iota(jnp.int32, (taken, pair), 1) < HD
    zero = jnp.zeros((taken, pair), BF16)

    def stacked(block):
        return jnp.concatenate(
            [jnp.where(first, block, zero), jnp.where(first, zero, block)], axis=0
        )

    d_query, d_key, d_value = [], [], []
    for keys, values, query, grad in (
        (keys_own, values_own, query_own, grad_own),
        (keys_peer, values_peer, query_peer, grad_peer),
    ):
        for p in range(width // pair):
            here = slice(p * pair, (p + 1) * pair)
            k, v = keys[:, here], values[:, here]
            q, g = stacked(query[:, here]), stacked(grad[:, here])
            scores = dot_nt(q, k)
            grown = jnp.exp2((scores - jnp.max(scores, axis=1, keepdims=True)) * EXPONENT)
            weights = grown / jnp.sum(grown, axis=1, keepdims=True)
            weights_grad = dot_nt(g, v)
            inner = jnp.sum(weights * weights_grad, axis=1, keepdims=True)
            scores_grad = (weights * (weights_grad - inner)).astype(BF16)
            d_value.append(dot_tn(weights.astype(BF16), g).astype(BF16))
            d_key.append((dot_tn(scores_grad, q) * factor).astype(BF16))
            split = dot(scores_grad, k) * factor
            d_query.append(jnp.where(first, split[:taken], split[taken:]).astype(BF16))
    half = len(d_key) // 2
    own = jnp.concatenate(d_key[:half] + d_value[:half], axis=1)
    mixed = jnp.concatenate([own] + d_key[half:] + d_value[half:], axis=1)
    query_part = jnp.concatenate(d_query, axis=1)
    query_own_part = query_part[:, :width]
    extra = back_one[...] + dot_nt(query_part, w_query[...])
    high = extra.astype(BF16)
    low = (extra - high.astype(F32)).astype(BF16)
    pick = picker(slots[...], length)
    tokens_grad[...] = dot_nt(mixed, w_key_value[...]) + dot_tn(
        jnp.concatenate([pick, pick], axis=0), jnp.concatenate([high, low], axis=0)
    )
    query_grads[pl.ds(pl.multiple_of(step * taken, taken), taken), :] = query_own_part
    update = dot_tn(tokens[...], own)
    query_sum = row_sum(query_own_part.astype(F32))
    value_sum = row_sum(own[:, width:].astype(F32))

    @pl.when(step == 0)
    def _():
        sums[...] = update
        grad_b_query[...] = query_sum
        grad_b_value[...] = value_sum

    @pl.when(step > 0)
    def _():
        sums[...] += update
        grad_b_query[...] += query_sum
        grad_b_value[...] += value_sum

    @pl.when(step == last)
    def _():
        grad_w_key_value[...] = sums[...].astype(BF16)
        grad_w_query[...] = dot_tn(picked_tokens[...], query_grads[...]).astype(BF16)


def attention_back(
    tokens, keys, values, query, grad, back_one, slots, picked_tokens, w_query, w_key_value, sequences
):
    rows, model = tokens.shape
    length = rows // sequences
    width = keys[0].shape[1]
    taken = slots.shape[0] // sequences
    shape = jax.ShapeDtypeStruct
    return pl.pallas_call(
        backward_body,
        grid=(sequences,),
        in_specs=[rows_spec(length, model)]
        + [rows_spec(length, width)] * 4
        + [rows_spec(taken, width)] * 4
        + [rows_spec(taken, model), rows_spec(taken, 1)]
        + [whole_spec(picked_tokens), whole_spec(w_query), whole_spec(w_key_value)],
        out_specs=[
            rows_spec(length, model),
            pl.BlockSpec((model, width), lambda i: (0, 0)),
            pl.BlockSpec((model, 2 * width), lambda i: (0, 0)),
            pl.BlockSpec((1, width), lambda i: (0, 0)),
            pl.BlockSpec((1, width), lambda i: (0, 0)),
        ],
        out_shape=[
            shape((rows, model), F32),
            shape((model, width), BF16),
            shape((model, 2 * width), BF16),
            shape((1, width), F32),
            shape((1, width), F32),
        ],
        scratch_shapes=[
            pltpu.VMEM((slots.shape[0], width), BF16),
            pltpu.VMEM((model, 2 * width), F32),
        ],
        compiler_params=params(),
        cost_estimate=pl.CostEstimate(
            flops=int(rows * model * 6 * 2 * width),
            bytes_accessed=rows * model * 14,
            transcendentals=0,
        ),
        name="attention_back",
    )(
        tokens,
        keys[0],
        keys[1],
        values[0],
        values[1],
        query[0],
        query[1],
        grad[0],
        grad[1],
        back_one,
        slots,
        picked_tokens,
        w_query,
        w_key_value,
    )


def dense_body(
    tokens,
    attended_own,
    attended_peer,
    w_out,
    w_up_own,
    w_up_peer,
    w_down_own,
    w_down_peer,
    b_out,
    gain_one,
    shift_one,
    b_up_own,
    b_up_peer,
    b_down,
    gain_two,
    shift_two,
    layer_out,
):
    attended = jnp.concatenate([attended_own[...], attended_peer[...]], axis=1)
    normed, _ = norm_parts(tokens[...].astype(F32) + dot(attended, w_out[...]) + b_out[...])
    layer_one = normed * gain_one[...] + shift_one[...]
    layer_low = layer_one.astype(BF16)
    summed = layer_one + b_down[...]
    for w_up, w_down, b_up in (
        (w_up_own, w_down_own, b_up_own),
        (w_up_peer, w_down_peer, b_up_peer),
    ):
        hidden = dot(layer_low, w_up[...]) + b_up[...]
        summed = summed + dot((hidden * gelu_share(hidden)).astype(BF16), w_down[...])
    normed, _ = norm_parts(summed)
    layer_out[...] = (normed * gain_two[...] + shift_two[...]).astype(BF16)


def dense_rows(*args):
    tokens, attended_own = args[0], args[1]
    rows, model = tokens.shape
    width = attended_own.shape[1]
    half = args[4].shape[1]
    block = 512
    return pl.pallas_call(
        dense_body,
        grid=(rows // block,),
        in_specs=[rows_spec(block, model), rows_spec(block, width), rows_spec(block, width)]
        + [whole_spec(array) for array in args[3:]],
        out_specs=rows_spec(block, model),
        out_shape=jax.ShapeDtypeStruct((rows, model), BF16),
        compiler_params=params(),
        cost_estimate=pl.CostEstimate(
            flops=int(rows * model * (8 * half + 4 * width)),
            bytes_accessed=rows * model * 6,
            transcendentals=rows * half * 2,
        ),
        name="dense",
    )(*args)


def on_device(
    tokens,
    out_grad,
    positions,
    w_query,
    b_query,
    w_key,
    w_value,
    b_value,
    w_out,
    b_out,
    gain_one,
    shift_one,
    w_up,
    b_up,
    w_down,
    b_down,
    gain_two,
    shift_two,
):
    sequences, picks = positions.shape
    model = tokens.shape[1]
    width = w_query.shape[1]
    half = w_up.shape[1]

    def peer(array):
        return lax.ppermute(array, "tensor", [(0, 1), (1, 0)])

    def row(vector):
        return vector.reshape(1, -1)

    earlier = jnp.tril(jnp.ones((picks, picks), jnp.bool_), -1)
    repeated = jnp.any((positions[:, :, None] == positions[:, None, :]) & earlier, axis=2)
    taken = -(-picks // 16) * 16
    slots = jnp.pad(
        jnp.where(repeated, -1, positions), ((0, 0), (0, taken - picks)), constant_values=-1
    ).reshape(-1, 1)

    qkv_own = jnp.concatenate([w_query, w_key, w_value], axis=1)
    qkv_peer = peer(qkv_own)
    biases_own = jnp.concatenate([b_query, b_value, b_up])
    biases_peer = peer(biases_own)
    out_peer = peer(w_out)
    up_peer = peer(w_up)
    down_peer = peer(w_down)
    b_up_peer = row(biases_peer[2 * width :])

    att_own, key_own, value_own, pick_q_own, pick_att_own = attention(
        tokens, qkv_own, row(b_query), row(b_value), slots, sequences
    )
    att_peer, key_peer, value_peer, pick_q_peer, pick_att_peer = attention(
        tokens,
        qkv_peer,
        row(biases_peer[:width]),
        row(biases_peer[width : 2 * width]),
        slots,
        sequences,
    )
    picked_tokens, picked_grad = pick_rows(tokens, out_grad, slots, sequences)
    out_all = jnp.concatenate([w_out, out_peer], axis=0)
    shared = (
        out_all,
        w_up,
        up_peer,
        w_down,
        down_peer,
        row(b_out),
        row(gain_one),
        row(shift_one),
        row(b_up),
        b_up_peer,
        row(b_down),
        row(gain_two),
    )
    (
        back_one,
        att_grad_own,
        att_grad_peer,
        grad_w_up,
        grad_w_down,
        grad_w_out,
        grad_b_up,
        vectors,
    ) = marked_rows(picked_tokens, pick_att_own, pick_att_peer, picked_grad, *shared)
    w_query_all = jnp.concatenate([w_query, qkv_peer[:, :width]], axis=1)
    w_key_value = jnp.concatenate([w_key, w_value, qkv_peer[:, width:]], axis=1)
    tokens_grad, grad_w_query, grad_w_key_value, grad_b_query, grad_b_value = attention_back(
        tokens,
        (key_own, key_peer),
        (value_own, value_peer),
        (pick_q_own, pick_q_peer),
        (att_grad_own, att_grad_peer),
        back_one,
        slots,
        picked_tokens,
        w_query_all,
        w_key_value,
        sequences,
    )
    layer_out = dense_rows(tokens, att_own, att_peer, *shared, row(shift_two))

    grad_w_up, grad_w_down, grad_w_out, grad_w_query, grad_w_key_value = lax.psum(
        (grad_w_up, grad_w_down, grad_w_out, grad_w_query, grad_w_key_value), "dp"
    )
    vectors, grad_b_up, grad_b_query, grad_b_value = lax.psum(
        (vectors, grad_b_up, grad_b_query, grad_b_value), "dp"
    )
    return (
        layer_out,
        tokens_grad,
        grad_w_query.astype(F32),
        grad_b_query[0],
        grad_w_key_value[:, :width].astype(F32),
        grad_w_key_value[:, width:].astype(F32),
        grad_b_value[0],
        grad_w_out.astype(F32),
        vectors[0],
        vectors[1],
        vectors[2],
        grad_w_up.astype(F32),
        grad_b_up[0],
        grad_w_down.astype(F32),
        vectors[3],
        vectors[4],
        vectors[5],
    )


def solution(mesh):
    across = P("dp", None)
    columns, rows, split, copied = P(None, "tensor"), P("tensor", None), P("tensor"), P()
    in_specs = (
        across,
        across,
        across,
        columns,
        split,
        columns,
        columns,
        split,
        rows,
        copied,
        copied,
        copied,
        columns,
        split,
        rows,
        copied,
        copied,
        copied,
    )
    out_specs = (
        across,
        across,
        columns,
        split,
        columns,
        columns,
        split,
        rows,
        copied,
        copied,
        copied,
        columns,
        split,
        rows,
        copied,
        copied,
        copied,
    )
    return jax.shard_map(
        on_device, mesh=mesh, in_specs=in_specs, out_specs=out_specs, check_vma=False
    )
```

time: 1440 us -> 495 us (0.34)
  waiting for transfers between devices: 738 us -> 145 us
  matrix products: 369 us -> 0 us
  Pallas kernels: 0 us -> 227 us
  local copies, waits for them, and re-layouts: 127 us -> 14.8 us
  other arithmetic: 121 us -> 17.9 us
    psum x5 -> x1, waiting for transfers between devices: 738 us -> 83.6 us  [on_device(): lax.psum((grad_w_up, grad_w_down, grad_w_out, grad_w_query, grad_w_key_va...]
    dot_general x74 -> x0, matrix products: 369 us -> none  [the longest x6 115 us: product(): return jnp.dot(left, right, preferred_element_type=jnp.float32)]
    pallas_call x0 -> x6, Pallas kernels: none -> 227 us  [the longest x1 65.1 us: dense_rows(): pl.pallas_call(dense_body, grid=(rows // block,), in_specs=[rows_spec(blo...]
    reduce_sum x17 -> x0, other arithmetic: 80.4 us -> none  [the longest x2 19.9 us: norm_parts(): average = jnp.mean(summed, axis=-1, keepdims=True)]
    ppermute x0 -> x5, waiting for transfers between devices: none -> 61.5 us  [peer(): return lax.ppermute(array, 'tensor', [(0, 1), (1, 0)])]
    dynamic_update_slice x40 -> x0, local copies, waits for them, and re-layouts: 37.4 us -> none  [on_device(): lax.map(attend, (by_heads(queries), by_heads(keys_low), by_heads(values_l...]
    unnamed x116 -> x47, local copies, waits for them, and re-layouts: 40.4 us -> 5.25 us
    while x6 -> x0, local copies, waits for them, and re-layouts: 20.4 us -> none  [the longest x3 12.3 us: on_device(): lax.map(attend_back, (by_heads(queries), by_heads(keys_low), by_heads(val...]
  transfers between devices with their start and end apart: 5 -> 6, of which waited for: 5 -> 3; matrix products, arithmetic and copies ran while one was open for 6% -> 4% of each run, Pallas kernels for 0% -> 28%
where the time goes in v1:
time: 495 us; the launch traced here: 488 us
  Pallas kernels  227 us (46%)
  waiting for transfers between devices  145 us (29%)
  blocking collectives  61.4 us (12%)
  other arithmetic  17.9 us (4%)
  local copies, waits for them, and re-layouts  14.8 us (3%)
  between operations  14.8 us (3%)
  starting transfers between devices  7.03 us (1%)
    psum x1, waiting for transfers between devices, on_device(): lax.psum((grad_w_up, grad_w_down, grad_w_out, grad_w_query, grad_w_key_va...  83.6 us
    pallas_call x1, Pallas kernels, dense_rows(): pl.pallas_call(dense_body, grid=(rows // block,), in_specs=[rows_spec(blo...  65.1 us
    pallas_call x1, Pallas kernels, attention_back(): pl.pallas_call(backward_body, grid=(sequences,), in_specs=[rows_spec(leng...  62.7 us
    ppermute x5, waiting for transfers between devices, peer(): return lax.ppermute(array, 'tensor', [(0, 1), (1, 0)])  61.5 us
    psum x1, blocking collectives, on_device(): lax.psum((vectors, grad_b_up, grad_b_query, grad_b_value), 'dp')  61.4 us
    pallas_call x2, Pallas kernels, attention(): pl.pallas_call(attention_body, grid=(sequences,), in_specs=[rows_spec(len...  61 us
    pallas_call x1, Pallas kernels, marked_rows(): pl.pallas_call(marked_body, out_shape=[shape((rows, model), F32), shape((...  28.9 us
  transfers between devices with their start and end apart: 6, of which 3 were waited for; matrix products, arithmetic and copies ran while one was open for 4% of the time, Pallas kernels for 28%

profile of v1, /device:TPU:0, one launch (start us, length us, event | category | flops | bytes accessed | tf_op | source)
XLA Modules:
  0.0 487.8 jit_solution(4061968004394437246)
XLA Ops:
  7.3 0.8 pad_maximum_fusion.2
  8.1 2.9 collective-permute-start.1
  11.1 1.9 constant_dynamic-update-slice_fusion.2
  13.0 1.9 constant_dynamic-update-slice_fusion.1
  14.9 0.9 constant_dynamic-update-slice_fusion.w_qkv
  15.8 2.0 collective-permute-start
  17.8 2.0 collective-permute-start.4
  21.1 1.5 and_reduce_fusion
  22.7 0.9 reshape.101.slots
  23.7 30.4 %attention.2 = (bf16[4096,384]{1,0:T(8,128)(2,1)}, bf16[4096,384]{1,0:T(8,128)(2,1)}, bf16[4096,384]{1,0:T(8,128)(2,1)}, bf16[640,384]{1,0:T(8,128)(2,1)}, bf16[640,384]{1,0:T(8,128)(2,1)}) custom-call(bf16[4096,768]{1,0:T(8,128)(2,1)} %tokens.9, bf16[768,1152]{1,0:T(8,128)(2,1)} %constant_dynamic-update-slice_fusion.w_qkv, f32[1,384]{1,0:T(1,128)} %reshape.88.b_query, ...), custom_call_target="tpu_custom_call" | custom-call | flops 20132659200 | bytes 15728640 | tf_op jit(solution)/shard_map/attention/pallas_call | solution.py:113
  55.3 0.6 reshape.94.gain_one
  56.5 0.6 reshape.98.b_down
  58.3 9.0 %pick.1 = (bf16[640,768]{1,0:T(8,128)(2,1)}, bf16[640,768]{1,0:T(8,128)(2,1)}) custom-call(bf16[4096,768]{1,0:T(8,128)(2,1)} %tokens.9, bf16[4096,768]{1,0:T(8,128)(2,1)} %out_grad.1, s32[640,1]{1,0:T(8,128)} %reshape.101.slots), custom_call_target="tpu_custom_call" | custom-call | tf_op jit(solution)/shard_map/pick/pallas_call | solution.py:145
  69.3 1.1 copy-done.4
  70.4 1.1 pad_maximum_fusion.1.w_query
  71.5 1.6 pad_maximum_fusion.w_key_value
  73.1 30.5 %attention.3 = (bf16[4096,384]{1,0:T(8,128)(2,1)}, bf16[4096,384]{1,0:T(8,128)(2,1)}, bf16[4096,384]{1,0:T(8,128)(2,1)}, bf16[640,384]{1,0:T(8,128)(2,1)}, bf16[640,384]{1,0:T(8,128)(2,1)}) custom-call(bf16[4096,768]{1,0:T(8,128)(2,1)} %tokens.9, bf16[768,1152]{1,0:T(8,128)(2,1)} %copy-done.5, f32[1,384]{1,0:T(1,128)} %reshape.91.b_query, ...), custom_call_target="tpu_custom_call" | custom-call | flops 20132659200 | bytes 15728640 | tf_op jit(solution)/shard_map/attention/pallas_call | solution.py:113
  103.6 12.4 %collective-permute-done.3.w_up_peer = bf16[768,1536]{1,0:T(8,128)(2,1)} collective-permute-done((bf16[768,1536]{1,0:T(8,128)(2,1)}, bf16[768,1536]{1,0:T(8,128)(2,1)}, u32[]{:S(2)}, u32[]{:S(2)}) %collective-permute-start.3) | collective-permute-done | bytes 2359328 | tf_op jit(solution)/shard_map/ppermute | solution.py:514
  116.0 49.1 %collective-permute-done.4.w_down_peer = bf16[1536,768]{1,0:T(8,128)(2,1)} collective-permute-done((bf16[1536,768]{1,0:T(8,128)(2,1)}, bf16[1536,768]{1,0:T(8,128)(2,1)}, u32[]{:S(2)}, u32[]{:S(2)}) %collective-permute-start.4) | collective-permute-done | bytes 2359328 | tf_op jit(solution)/shard_map/ppermute | solution.py:514
  165.1 28.9 %marked.1 = (f32[640,768]{1,0:T(8,128)}, bf16[640,384]{1,0:T(8,128)(2,1)}, bf16[640,384]{1,0:T(8,128)(2,1)}, bf16[768,1536]{1,0:T(8,128)(2,1)}, bf16[1536,768]{1...) custom-call(bf16[640,768]{1,0:T(8,128)(2,1)} %get-tuple-element.50.tokens.picked_tokens, ...), custom_call_target="tpu_custom_call" | custom-call | flops 16986931200 | bytes 14155776 | tf_op jit(solution)/shard_map/marked/pallas_call | solution.py:257
  194.1 62.7 %attention_back.1 = (f32[4096,768]{1,0:T(8,128)}, bf16[768,384]{1,0:T(8,128)(2,1)}, bf16[768,768]{1,0:T(8,128)(2,1)}, f32[1,384]{1,0:T(1,128)}, f32[1,384]{1,0:T(1,128)}) custom-call(bf16[4096,768]{1,0:T(8,128)(2,1)} %tokens.9, bf16[4096,384]{1,0:T(8,128)(2,1)} %get-tuple-element.44.keys_own, bf16[4096,384]{1,0:T(8,128)(2,1)} %get-tuple-element.45.keys_peer, ...), custom_call_target="tpu_custom_call" | custom-call | flops 14495514624 | bytes 44040192 | tf_op jit(solution)/shard_map/attention_back/pallas_call | solution.py:380
  256.8 0.7 reduce
  257.5 0.7 reduce.1
  258.2 61.4 %all-reduce.1 = (f32[384]{0:T(512)}, f32[384]{0:T(512)}, f32[8,768]{1,0:T(8,128)S(1)}, f32[1536]{0:T(1024)}) all-reduce(f32[384]{0:T(512)S(1)} %reduce, f32[384]{0:T(512)S(1)} %reduce.1, f32[8,768]{1,0:T(8,128)S(1)} %copy-done.10, f32[1536]{0:T(1024)S(1)} %reduce.5), channel_id=1, replica_groups=mesh['dp'=16,'tensor'=2] {'dp'}, use_global_device_ids=true, to_apply=%region_2.3 | all-reduce | flops 8448 | bytes 67584 | tf_op jit(solution)/shard_map/psum | solution.py:592
  319.6 0.6 slice_reduce_fusion
  320.3 65.1 %dense.1 = bf16[4096,768]{1,0:T(8,128)(2,1)} custom-call(bf16[4096,768]{1,0:T(8,128)(2,1)} %tokens.9, bf16[4096,384]{1,0:T(8,128)(2,1)} %get-tuple-element.42.attended_own, bf16[4096,384]{1,0:T(8,128)(2,1)} %get-tuple-element.43.attended_peer, bf16[768,768]{1,0:T(8,128)(2,1)} %copy-done.8, bf16[768,1536]{1,0:T(8,128)(2,1)} %w_up_own.3, ...), custom_call_target="tpu_custom_call" | custom-call | flops 43486543872 | bytes 18874368 | tf_op jit(solution)/shard_map/dense/pallas_call | solution.py:471
  385.4 83.6 %all-reduce.5.cloned.1.call-done = (bf16[768,384]{1,0:T(8,128)(2,1)}, bf16[768,768]{1,0:T(8,128)(2,1)}, bf16[384,768]{1,0:T(8,128)(2,1)}, bf16[768,1536]{1,0:T(8,128)(2,1)}, bf16[1536,768]{1,0:T(8,128)(2,1)}) async-done(((bf16[768,384]{1,0:T(8,128)(2,1)}, bf16[768,768]{1,0:T(8,128)(2,1)}, bf16[384,768]{1,0:T(8,128)(2,1)}, bf16[768,1536]{1,0:T(8,128)(2,1)}, bf16[1536,768]{1,0:T(8,128)(2,1)}), ...) | async-done | bytes 7077904 | tf_op jit(solution)/shard_map/psum | solution.py:589
  469.0 2.2 convert_element_type.18
  471.3 2.3 convert_element_type.21
  473.6 1.6 slice_convert_fusion
  475.1 2.8 convert_element_type.22
  477.9 2.5 convert_element_type.23
  (71 shorter events, 6.6 us)
Async XLA Ops:
  7.2 13.2 %copy-start.13 = (f32[384]{0:T(512)S(1)}, f32[384]{0:T(512)}, u32[]{:S(2)}) copy-start(f32[384]{0:T(512)} %param.25) | copy-start | bytes 4612
  7.2 12.6 %copy-start.12 = (f32[384]{0:T(512)S(1)}, f32[384]{0:T(512)}, u32[]{:S(2)}) copy-start(f32[384]{0:T(512)} %param.22) | copy-start | bytes 4612
  7.2 7.7 %copy-start.1 = (bf16[768,384]{1,0:T(8,128)(2,1)S(1)}, bf16[768,384]{1,0:T(8,128)(2,1)}, u32[]{:S(2)}) copy-start(bf16[768,384]{1,0:T(8,128)(2,1)} %param.24) | copy-start | bytes 1769476
  7.2 13.8 %copy-start.11 = (s32[8,76]{1,0:T(8,128)S(1)}, s32[8,76]{1,0:T(8,128)}, u32[]{:S(2)}) copy-start(s32[8,76]{1,0:T(8,128)} %param.20) | copy-start | bytes 7300
  7.2 461.8 %all-reduce.5.cloned.1.call-start = ((), (), s32[]{:S(2)}) async-start(), calls=%async_computation | async-start | bytes 14155776 | tf_op jit(solution)/shard_map/psum | solution.py:589
  8.1 59.3 %collective-permute-start.1 = (f32[2304]{0:T(1024)S(1)}, f32[2304]{0:T(1024)S(1)}, u32[]{:S(2)}, u32[]{:S(2)}) collective-permute-start(f32[2304]{0:T(1024)S(1)} %pad_maximum_fusion.2), channel_id=1, source_target_pairs={{0,1},{1,0},{2,3},{3,2},{4,5},{5,4},{6,7},{7,6},{8,9},{9,8},{10,11... | collective-permute-start | bytes 27656 | tf_op jit(solution)/shard_map/ppermute | solution.py:514
  11.0 58.1 %collective-permute-start.2 = (bf16[384,768]{1,0:T(8,128)(2,1)}, bf16[384,768]{1,0:T(8,128)(2,1)S(1)}, u32[]{:S(2)}, u32[]{:S(2)}) collective-permute-start(bf16[384,768]{1,0:T(8,128)(2,1)} %param.26), channel_id=1, source_target_pairs={{0,1},{1,0},{2,3},{3,2},{4,5},{5,4},{6,7},{7,6},{8,9},{9,8},{10,11... | collective-permute-start | bytes 1769480 | tf_op jit(solution)/shard_map/ppermute | solution.py:514
  15.8 53.3 %collective-permute-start = (bf16[768,1152]{1,0:T(8,128)(2,1)}, bf16[768,1152]{1,0:T(8,128)(2,1)S(1)}, u32[]{:S(2)}, u32[]{:S(2)}) collective-permute-start(bf16[768,1152]{1,0:T(8,128)(2,1)} %constant_dynamic-update-slice_fusion.w_qkv), channel_id=1, source_target_pairs={{0,1},{1,0},{2,3},{3,2},{4,5},{5,4},{6,7},{7,6},{8,9},{9,8},{10,11... | collective-permute-start | bytes 5308424 | tf_op jit(solution)/shard_map/ppermute | solution.py:514
  17.8 98.3 %collective-permute-start.3 = (bf16[768,1536]{1,0:T(8,128)(2,1)}, bf16[768,1536]{1,0:T(8,128)(2,1)}, u32[]{:S(2)}, u32[]{:S(2)}) collective-permute-start(bf16[768,1536]{1,0:T(8,128)(2,1)} %w_up_own.3), channel_id=1, source_target_pairs={{0,1},{1,0},{2,3},{3,2},{4,5},{5,4},{6,7},{7,6},{8,9},{9,8},{10,11... | collective-permute-start | bytes 7077896 | tf_op jit(solution)/shard_map/ppermute | solution.py:514
  17.8 147.3 %collective-permute-start.4 = (bf16[1536,768]{1,0:T(8,128)(2,1)}, bf16[1536,768]{1,0:T(8,128)(2,1)}, u32[]{:S(2)}, u32[]{:S(2)}) collective-permute-start(bf16[1536,768]{1,0:T(8,128)(2,1)} %w_down_own.3), channel_id=1, source_target_pairs={{0,1},{1,0},{2,3},{3,2},{4,5},{5,4},{6,7},{7,6},{8,9},{9,8},{10,11... | collective-permute-start | bytes 7077896 | tf_op jit(solution)/shard_map/ppermute | solution.py:514
  23.6 30.5 %copy-start.7 = (bf16[384,768]{1,0:T(8,128)(2,1)S(1)}, bf16[384,768]{1,0:T(8,128)(2,1)}, u32[]{:S(2)}) copy-start(bf16[384,768]{1,0:T(8,128)(2,1)} %param.26) | copy-start | bytes 1769476
  23.6 30.5 %copy-start.9 = (f32[1536]{0:T(1024)S(1)}, f32[1536]{0:T(1024)}, u32[]{:S(2)}) copy-start(f32[1536]{0:T(1024)} %param.31) | copy-start | bytes 18436
  23.6 31.1 %copy-start.15 = (f32[768]{0:T(1024)S(1)}, f32[768]{0:T(1024)}, u32[]{:S(2)}) copy-start(f32[768]{0:T(1024)} %param.27) | copy-start | bytes 9220
  23.6 31.7 %copy-start.16 = (f32[768]{0:T(1024)S(1)}, f32[768]{0:T(1024)}, u32[]{:S(2)}) copy-start(f32[768]{0:T(1024)} %param.28) | copy-start | bytes 9220
  23.6 32.3 %copy-start.17 = (f32[768]{0:T(1024)S(1)}, f32[768]{0:T(1024)}, u32[]{:S(2)}) copy-start(f32[768]{0:T(1024)} %param.29) | copy-start | bytes 9220
  23.6 32.9 %copy-start.18 = (f32[768]{0:T(1024)S(1)}, f32[768]{0:T(1024)}, u32[]{:S(2)}) copy-start(f32[768]{0:T(1024)} %param.33) | copy-start | bytes 9220
  23.6 33.5 %copy-start.19 = (f32[768]{0:T(1024)S(1)}, f32[768]{0:T(1024)}, u32[]{:S(2)}) copy-start(f32[768]{0:T(1024)} %param.34) | copy-start | bytes 9220
  23.6 34.1 %copy-start.20 = (f32[768]{0:T(1024)S(1)}, f32[768]{0:T(1024)}, u32[]{:S(2)}) copy-start(f32[768]{0:T(1024)} %param.35) | copy-start | bytes 9220
  69.0 1.3 copy-start.4
  69.1 2.4 copy-start.8
  69.1 2.4 copy-start.5
  69.2 2.3 copy-start
  194.1 64.1 %copy-start.14 = (f32[1,1536]{1,0:T(1,128)S(1)}, f32[1,1536]{1,0:T(1,128)}, u32[]{:S(2)}) copy-start(f32[1,1536]{1,0:T(1,128)} %get-tuple-element.65) | copy-start | bytes 18436
  194.1 64.1 %copy-start.10 = (f32[8,768]{1,0:T(8,128)S(1)}, f32[8,768]{1,0:T(8,128)}, u32[]{:S(2)}) copy-start(f32[8,768]{1,0:T(8,128)} %get-tuple-element.63) | copy-start | bytes 73732
  469.0 4.6 copy-start.6
  471.2 3.9 copy-start.3
  475.1 2.8 copy-start.2
Sparse Core Ops, SparseCore 0:
  320.4 148.5 all-reduce.4
